TPU v7x, 512 devices: a whole 4x4x16 slice. The times are simulated.
512 devices in a mesh: vocab: 32 (over x, y, core), dp: 16 (over z).
Axes of the slice: x: 4, y: 4, z: 16, core: 2. Of those that a mesh axis runs over, the one named last changes fastest.
Arguments:
- hidden: bfloat16 [2048, 2048], P('dp', 'vocab')
- head_weight: bfloat16 [2048, 65536], P('dp', 'vocab')
- teacher_logits: bfloat16 [2048, 65536], P('dp', 'vocab')
- target_ids: int32 [2048], P('dp'), may hold values from 0 to 65535
- segment_ids: int32 [16, 128], P('dp'), may hold values from 0 to 15, never falling along the last dimension, each value on 1 to 16 neighbouring positions
- pair_order: int32 [16, 16], P('dp'), may hold values from 0 to 15, each once within a row
Outputs:
- hidden_grad: bfloat16 [2048, 2048], P('dp', 'vocab')
- head_grad: float32 [2048, 65536], P('dp', 'vocab')
- loss: float32 [], replicated
Inputs may be any that keep to these rules, and one draw needn't show every extreme that they name: `segment_ids`: in each group the row's sequence number never falls along the rows, and every sequence has 1 to 16 rows. `pair_order`: each group's row is a permutation of its 16 sequences; pair p is entry 2p (chosen) and entry 2p + 1 (rejected).
All inputs are finite; a program needn't handle non-finite values.
Results may differ from a plain program's by a relative error of at most 0.018.
Values may be sent and summed in bfloat16 or wider, within the bound.
No kernel may reach another device: no remote copies, remote signals or barrier semaphores. Data moves between devices by JAX's collectives and lax.ppermute only.
A program may use at most 64 MiB of HBM per device.

v0:
```python
import jax
import jax.numpy as jnp
from jax import lax
from jax.sharding import PartitionSpec as P

dpo_beta = 0.1
dpo_gamma = 4.0


def pair_weights(log_ratio, segments, ordering):
    seq_count = ordering.shape[0]
    labels = lax.broadcasted_iota(jnp.int32, (1, seq_count), 1)
    seq_hot = (segments[:, None] == labels).astype(jnp.float32)
    seq_ratio = jnp.sum(seq_hot * log_ratio[:, None], axis=0)
    chosen = ordering[0::2]
    rejected = ordering[1::2]
    chosen_hot = (chosen[:, None] == labels).astype(jnp.float32)
    rejected_hot = (rejected[:, None] == labels).astype(jnp.float32)
    margin = dpo_beta * (
        jnp.sum(chosen_hot * seq_ratio[None, :], axis=1)
        - jnp.sum(rejected_hot * seq_ratio[None, :], axis=1)
    )
    strength = dpo_gamma * dpo_beta * jax.nn.sigmoid(-margin)
    coeffs = jnp.sum((rejected_hot - chosen_hot) * strength[:, None], axis=0)
    row_weight = jnp.sum(seq_hot * coeffs[None, :], axis=1)
    return (row_weight, jnp.sum(jax.nn.softplus(-margin)))


def to_all(block, axis):
    count = lax.axis_size(axis)
    copies = jnp.broadcast_to(block[None], (count,) + block.shape)
    return lax.all_to_all(copies, axis, 0, 0, tiled=True)


def on_device(hidden, head_weight, teacher_logits, target_ids, segment_ids, pair_order):
    f32, bf16 = (jnp.float32, jnp.bfloat16)
    rows_full = lax.all_gather(hidden, "vocab", axis=1, tiled=True)
    width = head_weight.shape[1]
    half = width // 2
    weight_lo = lax.all_gather(head_weight[:, :half], "dp", axis=0, tiled=True)
    weight_hi = lax.all_gather(head_weight[:, half:], "dp", axis=0, tiled=True)
    student = jnp.concatenate(
        [
            jnp.dot(rows_full, weight_lo, preferred_element_type=f32),
            jnp.dot(rows_full, weight_hi, preferred_element_type=f32),
        ],
        axis=1,
    )
    teacher = teacher_logits.astype(f32)
    n_vocab = lax.axis_size("vocab")
    n_dp = lax.axis_size("dp")
    rows = student.shape[0]
    offset = lax.axis_index("vocab") * width
    column = lax.broadcasted_iota(jnp.int32, student.shape, 1) + offset
    is_target = column == target_ids[:, None]
    own_max = jnp.max(student, axis=1)
    own_tmax = jnp.max(teacher, axis=1)
    own_exp = jnp.exp(student - own_max[:, None])
    own_texp = jnp.exp(teacher - own_tmax[:, None])
    stats = jnp.stack(
        [
            own_max,
            own_tmax,
            jnp.sum(own_exp, axis=1),
            jnp.sum(own_texp, axis=1),
            jnp.sum(own_texp * (teacher - student), axis=1),
            jnp.sum(jnp.where(is_target, student, 0.0), axis=1),
            jnp.sum(jnp.where(is_target, teacher, 0.0), axis=1),
            jnp.zeros((rows,), f32),
        ]
    )
    every = to_all(stats, "vocab").reshape(n_vocab, 8, rows)
    max_student = jnp.max(every[:, 0], axis=0)
    max_teacher = jnp.max(every[:, 1], axis=0)
    scale_s = jnp.exp(every[:, 0] - max_student[None])
    scale_t = jnp.exp(every[:, 1] - max_teacher[None])
    sum_student = jnp.sum(every[:, 2] * scale_s, axis=0)
    sum_teacher = jnp.sum(every[:, 3] * scale_t, axis=0)
    cross = jnp.sum(every[:, 4] * scale_t, axis=0)
    target_student = jnp.sum(every[:, 5], axis=0)
    target_teacher = jnp.sum(every[:, 6], axis=0)
    lse_student = max_student + jnp.log(sum_student)
    lse_teacher = max_teacher + jnp.log(sum_teacher)
    kl_rows = cross / sum_teacher - lse_teacher + lse_student
    log_ratio = target_student - lse_student - (target_teacher - lse_teacher)
    row_weight, dpo_sum = pair_weights(log_ratio, segment_ids[0], pair_order[0])
    group_objective = jnp.sum(kl_rows) + dpo_gamma * dpo_sum
    exp_student = jnp.exp(student - max_student[:, None])
    exp_teacher = jnp.exp(teacher - max_teacher[:, None])
    prob_student = exp_student / sum_student[:, None]
    prob_teacher = exp_teacher / sum_teacher[:, None]
    logit_grad = (
        prob_student - prob_teacher + row_weight[:, None] * (is_target.astype(f32) - prob_student)
    ).astype(bf16)
    grad_lo = logit_grad[:, :half]
    grad_hi = logit_grad[:, half:]
    all_lo = lax.all_gather(grad_lo, "dp", axis=0, tiled=True)
    all_hi = lax.all_gather(grad_hi, "dp", axis=0, tiled=True)
    nt = (((1,), (1,)), ((), ()))
    hidden_term = (
        lax.dot_general(grad_lo, weight_lo, nt, preferred_element_type=f32)
        + lax.dot_general(grad_hi, weight_hi, nt, preferred_element_type=f32)
    ).astype(bf16)
    feats = hidden_term.shape[1] // n_vocab
    terms = hidden_term.reshape(rows, n_vocab, feats).swapaxes(0, 1)
    terms = lax.all_to_all(terms, "vocab", 0, 0, tiled=True)
    hidden_grad = jnp.sum(terms.astype(f32), axis=0).astype(bf16)
    objectives = to_all(jnp.full((8, 128), group_objective, f32), "dp").reshape(n_dp, 8, 128)
    loss_value = jnp.sum(objectives[:, 0, 0]) / (rows * n_dp)
    grad_cols = lax.all_to_all(rows_full, "dp", split_axis=1, concat_axis=0, tiled=True)
    tn = (((0,), (0,)), ((), ()))
    head_grad = jnp.concatenate(
        [
            lax.dot_general(grad_cols, all_lo, tn, preferred_element_type=f32),
            lax.dot_general(grad_cols, all_hi, tn, preferred_element_type=f32),
        ],
        axis=1,
    )
    return (hidden_grad, head_grad, loss_value)


def solution(mesh):
    return jax.shard_map(
        on_device,
        mesh=mesh,
        in_specs=(
            P("dp", "vocab"),
            P("dp", "vocab"),
            P("dp", "vocab"),
            P("dp"),
            P("dp", None),
            P("dp", None),
        ),
        out_specs=(P("dp", "vocab"), P("dp", "vocab"), P()),
        check_vma=False,
    )
```

profile of v0, /device:TPU:2, one launch (start us, length us, event | category | flops | bytes accessed | tf_op | source)
XLA Modules:
  0.0 374.6 jit_solution(1377167011678018934)
XLA Ops:
  7.2 0.0 all-gather.5.cloned.1.call-start
  7.2 1.8 fusion.19
  9.0 0.0 all-gather.5.cloned.1.call-update
  9.1 0.0 all-gather.7.cloned.1.call-start
  9.1 0.7 all-gather.7.cloned.1.call-update
  9.8 1.2 reduce_max.71
  11.0 29.9 %all_gather.15 = bf16[128,2048]{0,1:T(8,128)(2,1)} all-gather(bf16[128,64]{0,1:T(8,128)(2,1)} %param.6), channel_id=1, replica_groups=mesh['vocab'=32,'dp'=16] {'vocab'}, dimensions={1}, use_global_device_ids=true | all-gather | bytes 540672 | tf_op jit(solution)/shard_map/all_gather | solution.py:37
  40.9 0.0 copy-start
  40.9 0.0 copy-start.1
  40.9 52.3 %all-gather.5.cloned.1.call-done = bf16[2048,1024]{1,0:T(8,128)(2,1)} async-done(((bf16[128,1024]{1,0:T(8,128)(2,1)}), bf16[2048,1024]{1,0:T(8,128)(2,1)}) %all-gather.5.cloned.1.call-update) | async-done | bytes 4194320 | tf_op jit(solution)/shard_map/all_gather | solution.py:40
  93.3 3.2 fusion.22
  96.4 0.0 copy-start.2
  96.5 0.0 copy-start.3
  96.5 74.8 %all-gather.7.cloned.1.call-done = bf16[2048,1024]{1,0:T(8,128)(2,1)} async-done(((bf16[128,1024]{1,0:T(8,128)(2,1)}), bf16[2048,1024]{1,0:T(8,128)(2,1)}) %all-gather.7.cloned.1.call-update) | async-done | bytes 4194320 | tf_op jit(solution)/shard_map/all_gather | solution.py:41
  171.3 3.2 fusion.23
  174.5 0.0 copy-done
  174.5 0.0 copy-done.1
  174.5 0.8 fusion.1
  175.4 0.7 broadcast_in_dim.8
  176.0 7.4 %all-to-all-start = ((f32[32,8,128]{2,1,0:T(8,128)}), f32[32,8,128]{2,1,0:T(8,128)S(1)}, u32[]{:S(2)}, u32[]{:S(2)}) async-start(f32[32,8,128]{2,1,0:T(8,128)} %broadcast_in_dim.8), calls=%async_computation | async-start | bytes 262144 | tf_op jit(solution)/shard_map/all_to_all | solution.py:32
  183.5 0.0 all-gather.9.cloned.1.call-start
  183.5 0.0 copy-done.2
  183.5 0.1 slice.51
  183.6 0.1 slice.50
  183.7 6.4 %all-to-all-done = f32[32,8,128]{2,1,0:T(8,128)S(1)} async-done(((f32[32,8,128]{2,1,0:T(8,128)}), f32[32,8,128]{2,1,0:T(8,128)S(1)}, u32[]{:S(2)}, u32[]{:S(2)}) %all-to-all-start) | async-done | bytes 131104 | tf_op jit(solution)/shard_map/all_to_all | solution.py:32
  190.1 0.1 fusion.20
  190.3 0.6 add_reduce_fusion
  190.9 0.0 copy-done.3
  190.9 0.1 select_reduce_fusion.1
  191.0 0.2 select_reduce_fusion.2
  191.3 0.6 fusion.14
  191.9 0.1 multiply_reduce_fusion.3
  192.0 0.1 select_reduce_fusion
  192.1 0.6 fusion.5
  192.7 0.9 fusion.18
  193.5 0.0 all-gather.9.cloned.1.call-update
  193.6 0.0 all-gather.11.cloned.1.call-start
  193.6 0.5 all-gather.11.cloned.1.call-update
  194.1 7.4 %all-to-all-start.2 = ((bf16[128,16,128]{0,2,1:T(8,128)(2,1)}), bf16[128,16,128]{0,2,1:T(8,128)(2,1)S(1)}, u32[]{:S(2)}, u32[]{:S(2)}) async-start(bf16[128,16,128]{0,2,1:T(8,128)(2,1)} %bitcast.17), calls=%async_computation.2 | async-start | bytes 1048576 | tf_op jit(solution)/shard_map/all_to_all | solution.py:110
  202.9 3.8 %fusion.16 = f32[128,2048]{1,0:T(8,128)S(1)} fusion(bf16[2048,1024]{1,0:T(8,128)(2,1)} %all-gather.5.cloned.1.call-done, bf16[128,2048]{1,0:T(8,128)(2,1)S(1)} %fusion.5), kind=kOutput, calls=%fused_computation.50 | convolution fusion | flops 536870912 | bytes 5505024 | tf_op jit(solution)/shard_map/dot_general | solution.py:101
  206.7 29.5 %all-to-all-done.2 = bf16[128,16,128]{0,2,1:T(8,128)(2,1)S(1)} async-done(((bf16[128,16,128]{0,2,1:T(8,128)(2,1)}), bf16[128,16,128]{0,2,1:T(8,128)(2,1)S(1)}, u32[]{:S(2)}, u32[]{:S(2)}) %all-to-all-start.2) | async-done | bytes 524320 | tf_op jit(solution)/shard_map/all_to_all | solution.py:110
  236.2 0.6 broadcast_in_dim_broadcast_in_dim_broadcast_in_dim.3
  236.8 6.4 %all-to-all-start.3 = ((f32[16,8,128]{2,1,0:T(8,128)}), f32[16,8,128]{2,1,0:T(8,128)S(1)}, u32[]{:S(2)}, u32[]{:S(2)}) async-start(f32[16,8,128]{2,1,0:T(8,128)} %broadcast_in_dim_broadcast_in_dim_broadcast_in_dim.3), calls=%async_computation.3 | async-start | bytes 131072 | tf_op jit(solution)/shard_map/all_to_all | solution.py:32
  243.2 3.7 fusion
  246.9 1.0 copy.32
  247.9 8.8 %all-to-all-done.3 = f32[16,8,128]{2,1,0:T(8,128)S(1)} async-done(((f32[16,8,128]{2,1,0:T(8,128)}), f32[16,8,128]{2,1,0:T(8,128)S(1)}, u32[]{:S(2)}, u32[]{:S(2)}) %all-to-all-start.3) | async-done | bytes 65568 | tf_op jit(solution)/shard_map/all_to_all | solution.py:32
  256.8 5.0 %all-to-all-start.1 = ((bf16[32,128,64]{1,2,0:T(8,128)(2,1)}), bf16[32,128,64]{1,2,0:T(8,128)(2,1)S(1)}, u32[]{:S(2)}, u32[]{:S(2)}) async-start(bf16[32,128,64]{1,2,0:T(8,128)(2,1)} %bitcast.16), calls=%async_computation.1 | async-start | bytes 1048576 | tf_op jit(solution)/shard_map/all_to_all | solution.py:106
  261.8 0.3 copy.33
  262.1 0.6 slice_reduce_fusion
  263.4 8.2 %all-to-all-done.1 = bf16[32,128,64]{1,2,0:T(8,128)(2,1)S(1)} async-done(((bf16[32,128,64]{1,2,0:T(8,128)(2,1)}), bf16[32,128,64]{1,2,0:T(8,128)(2,1)S(1)}, u32[]{:S(2)}, u32[]{:S(2)}) %all-to-all-start.1) | async-done | bytes 524320 | tf_op jit(solution)/shard_map/all_to_all | solution.py:106
  271.5 0.7 reduce_sum.188
  272.2 15.8 %all-gather.9.cloned.1.call-done = bf16[2048,1024]{1,0:T(8,128)(2,1)} async-done(((bf16[128,1024]{1,0:T(8,128)(2,1)}), bf16[2048,1024]{1,0:T(8,128)(2,1)}) %all-gather.9.cloned.1.call-update) | async-done | bytes 4194320 | tf_op jit(solution)/shard_map/all_gather | solution.py:97
  288.0 3.5 convolution_bitcast_fusion.1
  291.5 70.6 %all-gather.11.cloned.1.call-done = bf16[2048,1024]{1,0:T(8,128)(2,1)} async-done(((bf16[128,1024]{1,0:T(8,128)(2,1)}), bf16[2048,1024]{1,0:T(8,128)(2,1)}) %all-gather.11.cloned.1.call-update) | async-done | bytes 4194320 | tf_op jit(solution)/shard_map/all_gather | solution.py:98
  362.1 3.5 convolution_bitcast_fusion
  365.5 0.1 pad_maximum_fusion.1
  365.6 1.3 copy.35
  (10 shorter events, 0.2 us)
Async XLA Ops:
  7.2 86.1 %all-gather.5.cloned.1.call-start = ((), (), s32[]{:S(2)}) async-start(), calls=%async_computation.4 | async-start | bytes 4456448 | tf_op jit(solution)/shard_map/all_gather | solution.py:40
  9.1 162.2 %all-gather.7.cloned.1.call-start = ((), (), s32[]{:S(2)}) async-start(), calls=%async_computation.5 | async-start | bytes 4456448 | tf_op jit(solution)/shard_map/all_gather | solution.py:41
  40.9 133.6 %copy-start = (bf16[128,2048]{1,0:T(8,128)(2,1)S(1)}, bf16[128,2048]{1,0:T(8,128)(2,1)}, u32[]{:S(2)}) copy-start(bf16[128,2048]{1,0:T(8,128)(2,1)} %param.8) | copy-start | bytes 1572868
  40.9 133.6 %copy-start.1 = (s32[128]{0:T(128)S(1)}, s32[128]{0:T(128)}, u32[]{:S(2)}) copy-start(s32[128]{0:T(128)} %param.9) | copy-start | bytes 1540
  96.4 87.1 %copy-start.2 = (s32[1,16]{1,0:T(1,128)S(1)}, s32[1,16]{1,0:T(1,128)}, u32[]{:S(2)}) copy-start(s32[1,16]{1,0:T(1,128)} %param.11) | copy-start | bytes 196
  96.5 94.5 %copy-start.3 = (s32[1,128]{1,0:T(1,128)S(1)}, s32[1,128]{1,0:T(1,128)}, u32[]{:S(2)}) copy-start(s32[1,128]{1,0:T(1,128)} %param.10) | copy-start | bytes 1540
  176.0 14.1 %all-to-all-start = ((f32[32,8,128]{2,1,0:T(8,128)}), f32[32,8,128]{2,1,0:T(8,128)S(1)}, u32[]{:S(2)}, u32[]{:S(2)}) async-start(f32[32,8,128]{2,1,0:T(8,128)} %broadcast_in_dim.8), calls=%async_computation | async-start | bytes 262144 | tf_op jit(solution)/shard_map/all_to_all | solution.py:32
  183.5 104.5 %all-gather.9.cloned.1.call-start = ((), (), s32[]{:S(2)}) async-start(), calls=%async_computation.6 | async-start | bytes 4456448 | tf_op jit(solution)/shard_map/all_gather | solution.py:97
  193.6 168.5 %all-gather.11.cloned.1.call-start = ((), (), s32[]{:S(2)}) async-start(), calls=%async_computation.7 | async-start | bytes 4456448 | tf_op jit(solution)/shard_map/all_gather | solution.py:98
  194.1 42.0 %all-to-all-start.2 = ((bf16[128,16,128]{0,2,1:T(8,128)(2,1)}), bf16[128,16,128]{0,2,1:T(8,128)(2,1)S(1)}, u32[]{:S(2)}, u32[]{:S(2)}) async-start(bf16[128,16,128]{0,2,1:T(8,128)(2,1)} %bitcast.17), calls=%async_computation.2 | async-start | bytes 1048576 | tf_op jit(solution)/shard_map/all_to_all | solution.py:110
  236.8 20.0 %all-to-all-start.3 = ((f32[16,8,128]{2,1,0:T(8,128)}), f32[16,8,128]{2,1,0:T(8,128)S(1)}, u32[]{:S(2)}, u32[]{:S(2)}) async-start(f32[16,8,128]{2,1,0:T(8,128)} %broadcast_in_dim_broadcast_in_dim_broadcast_in_dim.3), calls=%async_computation.3 | async-start | bytes 131072 | tf_op jit(solution)/shard_map/all_to_all | solution.py:32
  256.8 14.8 %all-to-all-start.1 = ((bf16[32,128,64]{1,2,0:T(8,128)(2,1)}), bf16[32,128,64]{1,2,0:T(8,128)(2,1)S(1)}, u32[]{:S(2)}, u32[]{:S(2)}) async-start(bf16[32,128,64]{1,2,0:T(8,128)(2,1)} %bitcast.16), calls=%async_computation.1 | async-start | bytes 1048576 | tf_op jit(solution)/shard_map/all_to_all | solution.py:106
Sparse Core Ops, SparseCore 0:
  10.1 83.1 all-gather.4
  95.9 75.3 all-gather.6
  193.7 94.2 all-gather.8
  289.9 72.1 all-gather.10
where the time goes:
time: 375 us
  waiting for transfers between devices  268 us (71%)
  blocking collectives  29.9 us (8%)
  starting transfers between devices  26.5 us (7%)
  matrix products  20.8 us (6%)
  between operations  17 us (5%)
  local copies, waits for them, and re-layouts  6.89 us (2%)
  other arithmetic  5.88 us (2%)
    all_gather x1, waiting for transfers between devices, on_device(): weight_hi = lax.all_gather(head_weight[:, half:], 'dp', axis=0, tiled=True)  74.8 us
    all_gather x1, waiting for transfers between devices, on_device(): all_hi = lax.all_gather(grad_hi, 'dp', axis=0, tiled=True)  70.6 us
    all_gather x1, waiting for transfers between devices, on_device(): weight_lo = lax.all_gather(head_weight[:, :half], 'dp', axis=0, tiled=True)  52.3 us
    all_gather x1, blocking collectives, on_device(): rows_full = lax.all_gather(hidden, 'vocab', axis=1, tiled=True)  29.9 us
    all_to_all x1, waiting for transfers between devices, on_device(): lax.all_to_all(rows_full, 'dp', split_axis=1, concat_axis=0, tiled=True)  29.5 us
    all_gather x1, waiting for transfers between devices, on_device(): all_lo = lax.all_gather(grad_lo, 'dp', axis=0, tiled=True)  15.8 us
    all_to_all x2, waiting for transfers between devices, to_all(): return lax.all_to_all(copies, axis, 0, 0, tiled=True)  15.2 us
    all_to_all x2, starting transfers between devices, to_all(): return lax.all_to_all(copies, axis, 0, 0, tiled=True)  13.8 us
  transfers between devices with their start and end apart: 8, of which 8 were waited for; matrix products, arithmetic and copies ran while one was open for 5% of the time, Pallas kernels for 0%

commit v1 on v0

--- a/solution.py
+++ b/solution.py
@@ -5,6 +5,22 @@
 
 dpo_beta = 0.1
 dpo_gamma = 4.0
+
+
+def ring_gather(x, axis, dim):
+    ways, here, hop = (lax.axis_size(axis), lax.axis_index(axis), x.shape[dim])
+    shape = [n * ways if d == dim else n for d, n in enumerate(x.shape)]
+    full = lax.dynamic_update_slice_in_dim(jnp.zeros(shape, x.dtype), x, here * hop, axis=dim)
+    going_up = going_down = x
+    for far in range(1, ways // 2 + 1):
+        going_up = lax.ppermute(going_up, axis, [(d, (d + 1) % ways) for d in range(ways)])
+        full = lax.dynamic_update_slice_in_dim(full, going_up, (here - far) % ways * hop, axis=dim)
+        if 2 * far < ways:
+            going_down = lax.ppermute(going_down, axis, [(d, (d - 1) % ways) for d in range(ways)])
+            full = lax.dynamic_update_slice_in_dim(
+                full, going_down, (here + far) % ways * hop, axis=dim
+            )
+    return full
 
 
 def pair_weights(log_ratio, segments, ordering):
@@ -38,7 +54,7 @@
     width = head_weight.shape[1]
     half = width // 2
     weight_lo = lax.all_gather(head_weight[:, :half], "dp", axis=0, tiled=True)
-    weight_hi = lax.all_gather(head_weight[:, half:], "dp", axis=0, tiled=True)
+    weight_hi = ring_gather(head_weight[:, half:], "dp", 0)
     student = jnp.concatenate(
         [
             jnp.dot(rows_full, weight_lo, preferred_element_type=f32),

time: 375 us -> 346 us (0.923)
  the two profiles are of different devices: /device:TPU:2 before, /device:TPU:4 now
where the time goes in v1:
time: 346 us; the launch traced here: 345 us
  waiting for transfers between devices  171 us (49%)
  starting transfers between devices  84.2 us (24%)
  blocking collectives  27.1 us (8%)
  matrix products  21.2 us (6%)
  local copies, waits for them, and re-layouts  19.5 us (6%)
  between operations  17.5 us (5%)
  other arithmetic  4.84 us (1%)
    all_gather x1, waiting for transfers between devices, on_device(): all_lo = lax.all_gather(grad_lo, 'dp', axis=0, tiled=True)  72.7 us
    ppermute x7, starting transfers between devices, ring_gather(): lax.ppermute(going_down, axis, [(d, (d - 1) % ways) for d in range(ways)])  39.6 us
    ppermute x8, waiting for transfers between devices, ring_gather(): lax.ppermute(going_up, axis, [(d, (d + 1) % ways) for d in range(ways)])  31 us
    all_to_all x1, waiting for transfers between devices, on_device(): lax.all_to_all(rows_full, 'dp', split_axis=1, concat_axis=0, tiled=True)  29.4 us
    all_gather x1, blocking collectives, on_device(): rows_full = lax.all_gather(hidden, 'vocab', axis=1, tiled=True)  27.1 us
    ppermute x8, starting transfers between devices, ring_gather(): lax.ppermute(going_up, axis, [(d, (d + 1) % ways) for d in range(ways)])  17.2 us
    all_to_all x2, waiting for transfers between devices, to_all(): return lax.all_to_all(copies, axis, 0, 0, tiled=True)  14.4 us
    all_gather x1, waiting for transfers between devices, on_device(): all_hi = lax.all_gather(grad_hi, 'dp', axis=0, tiled=True)  13.8 us
  transfers between devices with their start and end apart: 22, of which 14 were waited for; matrix products, arithmetic and copies ran while one was open for 8% of the time, Pallas kernels for 0%

profile of v1, /device:TPU:4, one launch (start us, length us, event | category | flops | bytes accessed | tf_op | source)
XLA Modules:
  0.0 344.8 jit_solution(12150652068716133115)
XLA Ops:
  7.2 2.5 broadcast_in_dim.9
  9.7 0.9 fusion.19
  10.6 3.8 %collective-permute-start = (bf16[128,1024]{1,0:T(8,128)(2,1)S(1)}, bf16[128,1024]{1,0:T(8,128)(2,1)S(1)}, u32[]{:S(2)}, u32[]{:S(2)}) collective-permute-start(bf16[128,1024]{1,0:T(8,128)(2,1)S(1)} %get-tuple-element.29), channel_id=1, source_target_pairs={{0,1},{1,2},{2,3},{3,4},{4,5},{5,6},{6,7},{7,8},{8,9},{9,10},{10,1... | collective-permute-start | bytes 786440 | tf_op jit(solution)/shard_map/ppermute | solution.py:16
  14.5 9.5 %collective-permute-start.1 = (bf16[128,1024]{1,0:T(8,128)(2,1)S(1)}, bf16[128,1024]{1,0:T(8,128)(2,1)S(1)}, u32[]{:S(2)}, u32[]{:S(2)}) collective-permute-start(bf16[128,1024]{1,0:T(8,128)(2,1)S(1)} %get-tuple-element.29), channel_id=1, source_target_pairs={{0,15},{1,0},{2,1},{3,2},{4,3},{5,4},{6,5},{7,6},{8,7},{9,8},{10,9... | collective-permute-start | bytes 786440 | tf_op jit(solution)/shard_map/ppermute | solution.py:19
  24.0 4.4 %collective-permute-done = bf16[128,1024]{1,0:T(8,128)(2,1)S(1)} collective-permute-done((bf16[128,1024]{1,0:T(8,128)(2,1)S(1)}, bf16[128,1024]{1,0:T(8,128)(2,1)S(1)}, u32[]{:S(2)}, u32[]{:S(2)}) %collective-permute-start) | collective-permute-done | bytes 262176 | tf_op jit(solution)/shard_map/ppermute | solution.py:16
  28.4 1.9 collective-permute-start.2
  30.3 5.1 %collective-permute-start.3 = (bf16[128,1024]{1,0:T(8,128)(2,1)S(1)}, bf16[128,1024]{1,0:T(8,128)(2,1)S(1)}, u32[]{:S(2)}, u32[]{:S(2)}) collective-permute-start(bf16[128,1024]{1,0:T(8,128)(2,1)S(1)} %collective-permute-done.1), channel_id=1, source_target_pairs={{0,15},{1,0},{2,1},{3,2},{4,3},{5,4},{6,5},{7,6},{8,7},{9,8},{10,9... | collective-permute-start | bytes 786440 | tf_op jit(solution)/shard_map/ppermute | solution.py:19
  35.6 8.1 %collective-permute-done.2 = bf16[128,1024]{1,0:T(8,128)(2,1)S(1)} collective-permute-done((bf16[128,1024]{1,0:T(8,128)(2,1)S(1)}, bf16[128,1024]{1,0:T(8,128)(2,1)S(1)}, u32[]{:S(2)}, u32[]{:S(2)}) %collective-permute-start.2) | collective-permute-done | bytes 262176 | tf_op jit(solution)/shard_map/ppermute | solution.py:16
  43.7 1.9 collective-permute-start.4
  45.6 0.6 collective-permute-done.3
  46.3 4.5 %collective-permute-start.5 = (bf16[128,1024]{1,0:T(8,128)(2,1)S(1)}, bf16[128,1024]{1,0:T(8,128)(2,1)S(1)}, u32[]{:S(2)}, u32[]{:S(2)}) collective-permute-start(bf16[128,1024]{1,0:T(8,128)(2,1)S(1)} %collective-permute-done.3), channel_id=1, source_target_pairs={{0,15},{1,0},{2,1},{3,2},{4,3},{5,4},{6,5},{7,6},{8,7},{9,8},{10,9... | collective-permute-start | bytes 786440 | tf_op jit(solution)/shard_map/ppermute | solution.py:19
  50.8 27.1 %all_gather.12 = bf16[128,2048]{0,1:T(8,128)(2,1)} all-gather(bf16[128,64]{0,1:T(8,128)(2,1)S(1)} %copy-done.2), channel_id=1, replica_groups=mesh['vocab'=32,'dp'=16] {'vocab'}, dimensions={1}, use_global_device_ids=true | all-gather | bytes 540672 | tf_op jit(solution)/shard_map/all_gather | solution.py:53
  77.9 1.9 collective-permute-start.6
  80.1 0.7 constant_dynamic-update-slice_fusion.14
  80.9 5.1 %collective-permute-start.7 = (bf16[128,1024]{1,0:T(8,128)(2,1)S(1)}, bf16[128,1024]{1,0:T(8,128)(2,1)S(1)}, u32[]{:S(2)}, u32[]{:S(2)}) collective-permute-start(bf16[128,1024]{1,0:T(8,128)(2,1)S(1)} %collective-permute-done.5), channel_id=1, source_target_pairs={{0,15},{1,0},{2,1},{3,2},{4,3},{5,4},{6,5},{7,6},{8,7},{9,8},{10,9... | collective-permute-start | bytes 786440 | tf_op jit(solution)/shard_map/ppermute | solution.py:19
  86.0 0.7 constant_dynamic-update-slice_fusion.13
  86.7 8.4 %collective-permute-done.6 = bf16[128,1024]{1,0:T(8,128)(2,1)S(1)} collective-permute-done((bf16[128,1024]{1,0:T(8,128)(2,1)S(1)}, bf16[128,1024]{1,0:T(8,128)(2,1)S(1)}, u32[]{:S(2)}, u32[]{:S(2)}) %collective-permute-start.6) | collective-permute-done | bytes 262176 | tf_op jit(solution)/shard_map/ppermute | solution.py:16
  95.2 1.9 collective-permute-start.8
  97.1 0.7 constant_dynamic-update-slice_fusion.12
  97.8 0.7 constant_dynamic-update-slice_fusion.11
  98.6 5.1 %collective-permute-start.9 = (bf16[128,1024]{1,0:T(8,128)(2,1)S(1)}, bf16[128,1024]{1,0:T(8,128)(2,1)S(1)}, u32[]{:S(2)}, u32[]{:S(2)}) collective-permute-start(bf16[128,1024]{1,0:T(8,128)(2,1)S(1)} %collective-permute-done.7), channel_id=1, source_target_pairs={{0,15},{1,0},{2,1},{3,2},{4,3},{5,4},{6,5},{7,6},{8,7},{9,8},{10,9... | collective-permute-start | bytes 786440 | tf_op jit(solution)/shard_map/ppermute | solution.py:19
  103.7 0.7 constant_dynamic-update-slice_fusion.10
  104.4 2.7 collective-permute-done.8
  107.1 1.9 collective-permute-start.10
  109.0 0.7 constant_dynamic-update-slice_fusion.9
  109.7 0.7 constant_dynamic-update-slice_fusion.8
  110.5 5.1 %collective-permute-start.11 = (bf16[128,1024]{1,0:T(8,128)(2,1)S(1)}, bf16[128,1024]{1,0:T(8,128)(2,1)S(1)}, u32[]{:S(2)}, u32[]{:S(2)}) collective-permute-start(bf16[128,1024]{1,0:T(8,128)(2,1)S(1)} %collective-permute-done.9), channel_id=1, source_target_pairs={{0,15},{1,0},{2,1},{3,2},{4,3},{5,4},{6,5},{7,6},{8,7},{9,8},{10,9... | collective-permute-start | bytes 786440 | tf_op jit(solution)/shard_map/ppermute | solution.py:19
  115.6 0.7 constant_dynamic-update-slice_fusion.7
  116.3 1.5 collective-permute-done.10
  117.8 1.9 collective-permute-start.12
  119.7 0.7 constant_dynamic-update-slice_fusion.6
  120.4 0.7 constant_dynamic-update-slice_fusion.5
  121.1 5.1 %collective-permute-start.13 = (bf16[128,1024]{1,0:T(8,128)(2,1)S(1)}, bf16[128,1024]{1,0:T(8,128)(2,1)S(1)}, u32[]{:S(2)}, u32[]{:S(2)}) collective-permute-start(bf16[128,1024]{1,0:T(8,128)(2,1)S(1)} %collective-permute-done.11), channel_id=1, source_target_pairs={{0,15},{1,0},{2,1},{3,2},{4,3},{5,4},{6,5},{7,6},{8,7},{9,8},{10,9... | collective-permute-start | bytes 786440 | tf_op jit(solution)/shard_map/ppermute | solution.py:19
  126.3 0.7 constant_dynamic-update-slice_fusion.4
  127.6 1.9 collective-permute-start.14
  129.5 0.7 constant_dynamic-update-slice_fusion.3
  130.2 0.7 constant_dynamic-update-slice_fusion.2
  130.9 0.7 constant_dynamic-update-slice_fusion.1
  131.7 5.4 %collective-permute-done.14 = bf16[128,1024]{1,0:T(8,128)(2,1)S(1)} collective-permute-done((bf16[128,1024]{1,0:T(8,128)(2,1)S(1)}, bf16[128,1024]{1,0:T(8,128)(2,1)S(1)}, u32[]{:S(2)}, u32[]{:S(2)}) %collective-permute-start.14) | collective-permute-done | bytes 262176 | tf_op jit(solution)/shard_map/ppermute | solution.py:16
  137.0 0.7 constant_dynamic-update-slice_fusion
  137.8 3.6 %fusion.23 = (f32[128]{0:T(128)S(1)}, f32[1024,128]{1,0:T(8,128)S(1)}) fusion(bf16[2048,1024]{1,0:T(8,128)(2,1)} %constant_dynamic-update-slice_fusion, bf16[128,2048]{0,1:T(8,128)(2,1)} %all_gather.12), kind=kOutput, calls=%fused_computation.73 | convolution fusion | flops 537001856 | bytes 5243392 | tf_op jit(solution)/shard_map/dot_general | solution.py:61
  141.6 3.2 fusion.22
  144.8 0.8 fusion.1
  145.7 0.7 broadcast_in_dim.11
  146.3 5.8 %all-to-all-start = ((f32[32,8,128]{2,1,0:T(8,128)}), f32[32,8,128]{2,1,0:T(8,128)S(1)}, u32[]{:S(2)}, u32[]{:S(2)}) async-start(f32[32,8,128]{2,1,0:T(8,128)} %broadcast_in_dim.11), calls=%async_computation | async-start | bytes 262144 | tf_op jit(solution)/shard_map/all_to_all | solution.py:48
  152.4 5.6 %all-to-all-done = f32[32,8,128]{2,1,0:T(8,128)S(1)} async-done(((f32[32,8,128]{2,1,0:T(8,128)}), f32[32,8,128]{2,1,0:T(8,128)S(1)}, u32[]{:S(2)}, u32[]{:S(2)}) %all-to-all-start) | async-done | bytes 131104 | tf_op jit(solution)/shard_map/all_to_all | solution.py:48
  159.1 0.6 fusion.14
  160.5 0.8 fusion.18
  161.5 0.7 all-gather.6.cloned.1.call-update
  162.2 8.7 %all-to-all-start.2 = ((bf16[128,16,128]{0,2,1:T(8,128)(2,1)}), bf16[128,16,128]{0,2,1:T(8,128)(2,1)S(1)}, u32[]{:S(2)}, u32[]{:S(2)}) async-start(bf16[128,16,128]{0,2,1:T(8,128)(2,1)} %bitcast.18), calls=%async_computation.2 | async-start | bytes 1048576 | tf_op jit(solution)/shard_map/all_to_all | solution.py:126
  172.1 3.8 %fusion.16 = f32[128,2048]{1,0:T(8,128)S(1)} fusion(bf16[2048,1024]{1,0:T(8,128)(2,1)} %all-gather.4.cloned.1.call-done, bf16[128,2048]{1,0:T(8,128)(2,1)S(1)} %fusion.5), kind=kOutput, calls=%fused_computation.66 | convolution fusion | flops 536870912 | bytes 5505024 | tf_op jit(solution)/shard_map/dot_general | solution.py:117
  175.9 29.4 %all-to-all-done.2 = bf16[128,16,128]{0,2,1:T(8,128)(2,1)S(1)} async-done(((bf16[128,16,128]{0,2,1:T(8,128)(2,1)}), bf16[128,16,128]{0,2,1:T(8,128)(2,1)S(1)}, u32[]{:S(2)}, u32[]{:S(2)}) %all-to-all-start.2) | async-done | bytes 524320 | tf_op jit(solution)/shard_map/all_to_all | solution.py:126
  205.9 6.4 %all-to-all-start.3 = ((f32[16,8,128]{2,1,0:T(8,128)}), f32[16,8,128]{2,1,0:T(8,128)S(1)}, u32[]{:S(2)}, u32[]{:S(2)}) async-start(f32[16,8,128]{2,1,0:T(8,128)} %broadcast_in_dim_broadcast_in_dim_broadcast_in_dim.3), calls=%async_computation.3 | async-start | bytes 131072 | tf_op jit(solution)/shard_map/all_to_all | solution.py:48
  212.4 3.7 %fusion = bf16[128,2048]{1,0:T(8,128)(2,1)S(1)} fusion(f32[128,2048]{1,0:T(8,128)S(1)} %fusion.16, bf16[2048,1024]{1,0:T(8,128)(2,1)} %constant_dynamic-update-slice_fusion, bf16[128,2048]{1,0:T(8,128)(2,1)S(1)} %fusion.5), kind=kOutput, calls=%fused_computation.1 | convolution fusion | flops 537395200 | bytes 6029312 | tf_op jit(solution)/shard_map/dot_general | solution.py:118
  216.1 1.0 copy.37
  217.1 8.8 %all-to-all-done.3 = f32[16,8,128]{2,1,0:T(8,128)S(1)} async-done(((f32[16,8,128]{2,1,0:T(8,128)}), f32[16,8,128]{2,1,0:T(8,128)S(1)}, u32[]{:S(2)}, u32[]{:S(2)}) %all-to-all-start.3) | async-done | bytes 65568 | tf_op jit(solution)/shard_map/all_to_all | solution.py:48
  225.9 6.3 %all-to-all-start.1 = ((bf16[32,128,64]{1,2,0:T(8,128)(2,1)}), bf16[32,128,64]{1,2,0:T(8,128)(2,1)S(1)}, u32[]{:S(2)}, u32[]{:S(2)}) async-start(bf16[32,128,64]{1,2,0:T(8,128)(2,1)} %bitcast.17), calls=%async_computation.1 | async-start | bytes 1048576 | tf_op jit(solution)/shard_map/all_to_all | solution.py:122
  233.8 7.9 %all-to-all-done.1 = bf16[32,128,64]{1,2,0:T(8,128)(2,1)S(1)} async-done(((bf16[32,128,64]{1,2,0:T(8,128)(2,1)}), bf16[32,128,64]{1,2,0:T(8,128)(2,1)S(1)}, u32[]{:S(2)}, u32[]{:S(2)}) %all-to-all-start.1) | async-done | bytes 524320 | tf_op jit(solution)/shard_map/all_to_all | solution.py:122
  241.7 0.7 reduce_sum.188
  242.4 13.8 %all-gather.8.cloned.1.call-done = bf16[2048,1024]{1,0:T(8,128)(2,1)} async-done(((bf16[128,1024]{1,0:T(8,128)(2,1)}), bf16[2048,1024]{1,0:T(8,128)(2,1)}) %all-gather.8.cloned.1.call-update) | async-done | bytes 4194320 | tf_op jit(solution)/shard_map/all_gather | solution.py:114
  256.2 3.5 %convolution_bitcast_fusion = f32[128,1024]{0,1:T(8,128)S(1)} fusion(bf16[2048,1024]{1,0:T(8,128)(2,1)} %all-gather.8.cloned.1.call-done, bf16[2048,128]{1,0:T(8,128)(2,1)S(1)} %bitcast.46), kind=kOutput, calls=%fused_computation.8 | convolution fusion | flops 536870912 | bytes 5242880 | tf_op jit(solution)/shard_map/dot_general | solution.py:131
  259.7 72.7 %all-gather.6.cloned.1.call-done = bf16[2048,1024]{1,0:T(8,128)(2,1)} async-done(((bf16[128,1024]{1,0:T(8,128)(2,1)}), bf16[2048,1024]{1,0:T(8,128)(2,1)}) %all-gather.6.cloned.1.call-update) | async-done | bytes 4194320 | tf_op jit(solution)/shard_map/all_gather | solution.py:113
  332.3 3.5 %convolution_bitcast_fusion.1 = f32[128,1024]{0,1:T(8,128)S(1)} fusion(bf16[2048,1024]{1,0:T(8,128)(2,1)} %all-gather.6.cloned.1.call-done, bf16[2048,128]{1,0:T(8,128)(2,1)S(1)} %bitcast.47), kind=kOutput, calls=%fused_computation.9 | convolution fusion | flops 536870912 | bytes 5242880 | tf_op jit(solution)/shard_map/dot_general | solution.py:130
  335.9 1.3 copy.40
  (51 shorter events, 4.9 us)
Async XLA Ops:
  7.2 2.6 copy-start.1
  7.2 28.2 %copy-start = (bf16[128,2048]{1,0:T(8,128)(2,1)S(1)}, bf16[128,2048]{1,0:T(8,128)(2,1)}, u32[]{:S(2)}) copy-start(bf16[128,2048]{1,0:T(8,128)(2,1)} %param.8) | copy-start | bytes 1572868
  7.2 43.6 %copy-start.2 = (bf16[128,64]{0,1:T(8,128)(2,1)S(1)}, bf16[128,64]{0,1:T(8,128)(2,1)}, u32[]{:S(2)}) copy-start(bf16[128,64]{0,1:T(8,128)(2,1)} %param.6) | copy-start | bytes 49156
  7.2 134.4 %all-gather.4.cloned.1.call-start = ((), (), s32[]{:S(2)}) async-start(), calls=%async_computation.4 | async-start | bytes 4456448 | tf_op jit(solution)/shard_map/all_gather | solution.py:56
  10.6 17.7 %collective-permute-start = (bf16[128,1024]{1,0:T(8,128)(2,1)S(1)}, bf16[128,1024]{1,0:T(8,128)(2,1)S(1)}, u32[]{:S(2)}, u32[]{:S(2)}) collective-permute-start(bf16[128,1024]{1,0:T(8,128)(2,1)S(1)} %get-tuple-element.29), channel_id=1, source_target_pairs={{0,1},{1,2},{2,3},{3,4},{4,5},{5,6},{6,7},{7,8},{8,9},{9,10},{10,1... | collective-permute-start | bytes 786440 | tf_op jit(solution)/shard_map/ppermute | solution.py:16
  14.5 15.8 %collective-permute-start.1 = (bf16[128,1024]{1,0:T(8,128)(2,1)S(1)}, bf16[128,1024]{1,0:T(8,128)(2,1)S(1)}, u32[]{:S(2)}, u32[]{:S(2)}) collective-permute-start(bf16[128,1024]{1,0:T(8,128)(2,1)S(1)} %get-tuple-element.29), channel_id=1, source_target_pairs={{0,15},{1,0},{2,1},{3,2},{4,3},{5,4},{6,5},{7,6},{8,7},{9,8},{10,9... | collective-permute-start | bytes 786440 | tf_op jit(solution)/shard_map/ppermute | solution.py:19
  28.4 15.3 %collective-permute-start.2 = (bf16[128,1024]{1,0:T(8,128)(2,1)S(1)}, bf16[128,1024]{1,0:T(8,128)(2,1)S(1)}, u32[]{:S(2)}, u32[]{:S(2)}) collective-permute-start(bf16[128,1024]{1,0:T(8,128)(2,1)S(1)} %collective-permute-done), channel_id=1, source_target_pairs={{0,1},{1,2},{2,3},{3,4},{4,5},{5,6},{6,7},{7,8},{8,9},{9,10},{10,1... | collective-permute-start | bytes 786440 | tf_op jit(solution)/shard_map/ppermute | solution.py:16
  30.3 16.0 %collective-permute-start.3 = (bf16[128,1024]{1,0:T(8,128)(2,1)S(1)}, bf16[128,1024]{1,0:T(8,128)(2,1)S(1)}, u32[]{:S(2)}, u32[]{:S(2)}) collective-permute-start(bf16[128,1024]{1,0:T(8,128)(2,1)S(1)} %collective-permute-done.1), channel_id=1, source_target_pairs={{0,15},{1,0},{2,1},{3,2},{4,3},{5,4},{6,5},{7,6},{8,7},{9,8},{10,9... | collective-permute-start | bytes 786440 | tf_op jit(solution)/shard_map/ppermute | solution.py:19
  43.7 34.2 %collective-permute-start.4 = (bf16[128,1024]{1,0:T(8,128)(2,1)S(1)}, bf16[128,1024]{1,0:T(8,128)(2,1)S(1)}, u32[]{:S(2)}, u32[]{:S(2)}) collective-permute-start(bf16[128,1024]{1,0:T(8,128)(2,1)S(1)} %collective-permute-done.2), channel_id=1, source_target_pairs={{0,1},{1,2},{2,3},{3,4},{4,5},{5,6},{6,7},{7,8},{8,9},{9,10},{10,1... | collective-permute-start | bytes 786440 | tf_op jit(solution)/shard_map/ppermute | solution.py:16
  46.3 34.6 %collective-permute-start.5 = (bf16[128,1024]{1,0:T(8,128)(2,1)S(1)}, bf16[128,1024]{1,0:T(8,128)(2,1)S(1)}, u32[]{:S(2)}, u32[]{:S(2)}) collective-permute-start(bf16[128,1024]{1,0:T(8,128)(2,1)S(1)} %collective-permute-done.3), channel_id=1, source_target_pairs={{0,15},{1,0},{2,1},{3,2},{4,3},{5,4},{6,5},{7,6},{8,7},{9,8},{10,9... | collective-permute-start | bytes 786440 | tf_op jit(solution)/shard_map/ppermute | solution.py:19
  77.9 17.2 %collective-permute-start.6 = (bf16[128,1024]{1,0:T(8,128)(2,1)S(1)}, bf16[128,1024]{1,0:T(8,128)(2,1)S(1)}, u32[]{:S(2)}, u32[]{:S(2)}) collective-permute-start(bf16[128,1024]{1,0:T(8,128)(2,1)S(1)} %collective-permute-done.4), channel_id=1, source_target_pairs={{0,1},{1,2},{2,3},{3,4},{4,5},{5,6},{6,7},{7,8},{8,9},{9,10},{10,1... | collective-permute-start | bytes 786440 | tf_op jit(solution)/shard_map/ppermute | solution.py:16
  80.9 17.7 %collective-permute-start.7 = (bf16[128,1024]{1,0:T(8,128)(2,1)S(1)}, bf16[128,1024]{1,0:T(8,128)(2,1)S(1)}, u32[]{:S(2)}, u32[]{:S(2)}) collective-permute-start(bf16[128,1024]{1,0:T(8,128)(2,1)S(1)} %collective-permute-done.5), channel_id=1, source_target_pairs={{0,15},{1,0},{2,1},{3,2},{4,3},{5,4},{6,5},{7,6},{8,7},{9,8},{10,9... | collective-permute-start | bytes 786440 | tf_op jit(solution)/shard_map/ppermute | solution.py:19
  95.2 11.9 %collective-permute-start.8 = (bf16[128,1024]{1,0:T(8,128)(2,1)S(1)}, bf16[128,1024]{1,0:T(8,128)(2,1)S(1)}, u32[]{:S(2)}, u32[]{:S(2)}) collective-permute-start(bf16[128,1024]{1,0:T(8,128)(2,1)S(1)} %collective-permute-done.6), channel_id=1, source_target_pairs={{0,1},{1,2},{2,3},{3,4},{4,5},{5,6},{6,7},{7,8},{8,9},{9,10},{10,1... | collective-permute-start | bytes 786440 | tf_op jit(solution)/shard_map/ppermute | solution.py:16
  98.6 11.9 %collective-permute-start.9 = (bf16[128,1024]{1,0:T(8,128)(2,1)S(1)}, bf16[128,1024]{1,0:T(8,128)(2,1)S(1)}, u32[]{:S(2)}, u32[]{:S(2)}) collective-permute-start(bf16[128,1024]{1,0:T(8,128)(2,1)S(1)} %collective-permute-done.7), channel_id=1, source_target_pairs={{0,15},{1,0},{2,1},{3,2},{4,3},{5,4},{6,5},{7,6},{8,7},{9,8},{10,9... | collective-permute-start | bytes 786440 | tf_op jit(solution)/shard_map/ppermute | solution.py:19
  107.1 10.7 %collective-permute-start.10 = (bf16[128,1024]{1,0:T(8,128)(2,1)S(1)}, bf16[128,1024]{1,0:T(8,128)(2,1)S(1)}, u32[]{:S(2)}, u32[]{:S(2)}) collective-permute-start(bf16[128,1024]{1,0:T(8,128)(2,1)S(1)} %collective-permute-done.8), channel_id=1, source_target_pairs={{0,1},{1,2},{2,3},{3,4},{4,5},{5,6},{6,7},{7,8},{8,9},{9,10},{10,1... | collective-permute-start | bytes 786440 | tf_op jit(solution)/shard_map/ppermute | solution.py:16
  110.5 10.7 %collective-permute-start.11 = (bf16[128,1024]{1,0:T(8,128)(2,1)S(1)}, bf16[128,1024]{1,0:T(8,128)(2,1)S(1)}, u32[]{:S(2)}, u32[]{:S(2)}) collective-permute-start(bf16[128,1024]{1,0:T(8,128)(2,1)S(1)} %collective-permute-done.9), channel_id=1, source_target_pairs={{0,15},{1,0},{2,1},{3,2},{4,3},{5,4},{6,5},{7,6},{8,7},{9,8},{10,9... | collective-permute-start | bytes 786440 | tf_op jit(solution)/shard_map/ppermute | solution.py:19
  117.8 9.8 %collective-permute-start.12 = (bf16[128,1024]{1,0:T(8,128)(2,1)S(1)}, bf16[128,1024]{1,0:T(8,128)(2,1)S(1)}, u32[]{:S(2)}, u32[]{:S(2)}) collective-permute-start(bf16[128,1024]{1,0:T(8,128)(2,1)S(1)} %collective-permute-done.10), channel_id=1, source_target_pairs={{0,1},{1,2},{2,3},{3,4},{4,5},{5,6},{6,7},{7,8},{8,9},{9,10},{10,1... | collective-permute-start | bytes 786440 | tf_op jit(solution)/shard_map/ppermute | solution.py:16
  121.1 9.8 %collective-permute-start.13 = (bf16[128,1024]{1,0:T(8,128)(2,1)S(1)}, bf16[128,1024]{1,0:T(8,128)(2,1)S(1)}, u32[]{:S(2)}, u32[]{:S(2)}) collective-permute-start(bf16[128,1024]{1,0:T(8,128)(2,1)S(1)} %collective-permute-done.11), channel_id=1, source_target_pairs={{0,15},{1,0},{2,1},{3,2},{4,3},{5,4},{6,5},{7,6},{8,7},{9,8},{10,9... | collective-permute-start | bytes 786440 | tf_op jit(solution)/shard_map/ppermute | solution.py:19
  127.6 9.5 %collective-permute-start.14 = (bf16[128,1024]{1,0:T(8,128)(2,1)S(1)}, bf16[128,1024]{1,0:T(8,128)(2,1)S(1)}, u32[]{:S(2)}, u32[]{:S(2)}) collective-permute-start(bf16[128,1024]{1,0:T(8,128)(2,1)S(1)} %collective-permute-done.12), channel_id=1, source_target_pairs={{0,1},{1,2},{2,3},{3,4},{4,5},{5,6},{6,7},{7,8},{8,9},{9,10},{10,1... | collective-permute-start | bytes 786440 | tf_op jit(solution)/shard_map/ppermute | solution.py:16
  141.3 3.5 %copy-start.3 = (s32[128]{0:T(128)S(1)}, s32[128]{0:T(128)}, u32[]{:S(2)}) copy-start(s32[128]{0:T(128)} %param.9) | copy-start | bytes 1540
  141.4 10.8 %copy-start.4 = (s32[1,16]{1,0:T(1,128)S(1)}, s32[1,16]{1,0:T(1,128)}, u32[]{:S(2)}) copy-start(s32[1,16]{1,0:T(1,128)} %param.11) | copy-start | bytes 196
  141.4 17.4 %copy-start.5 = (s32[1,128]{1,0:T(1,128)S(1)}, s32[1,128]{1,0:T(1,128)}, u32[]{:S(2)}) copy-start(s32[1,128]{1,0:T(1,128)} %param.10) | copy-start | bytes 1540
  146.3 11.7 %all-to-all-start = ((f32[32,8,128]{2,1,0:T(8,128)}), f32[32,8,128]{2,1,0:T(8,128)S(1)}, u32[]{:S(2)}, u32[]{:S(2)}) async-start(f32[32,8,128]{2,1,0:T(8,128)} %broadcast_in_dim.11), calls=%async_computation | async-start | bytes 262144 | tf_op jit(solution)/shard_map/all_to_all | solution.py:48
  152.2 104.0 %all-gather.8.cloned.1.call-start = ((), (), s32[]{:S(2)}) async-start(), calls=%async_computation.6 | async-start | bytes 4456448 | tf_op jit(solution)/shard_map/all_gather | solution.py:114
  161.4 170.9 %all-gather.6.cloned.1.call-start = ((), (), s32[]{:S(2)}) async-start(), calls=%async_computation.5 | async-start | bytes 4456448 | tf_op jit(solution)/shard_map/all_gather | solution.py:113
  162.2 43.2 %all-to-all-start.2 = ((bf16[128,16,128]{0,2,1:T(8,128)(2,1)}), bf16[128,16,128]{0,2,1:T(8,128)(2,1)S(1)}, u32[]{:S(2)}, u32[]{:S(2)}) async-start(bf16[128,16,128]{0,2,1:T(8,128)(2,1)} %bitcast.18), calls=%async_computation.2 | async-start | bytes 1048576 | tf_op jit(solution)/shard_map/all_to_all | solution.py:126
  205.9 20.0 %all-to-all-start.3 = ((f32[16,8,128]{2,1,0:T(8,128)}), f32[16,8,128]{2,1,0:T(8,128)S(1)}, u32[]{:S(2)}, u32[]{:S(2)}) async-start(f32[16,8,128]{2,1,0:T(8,128)} %broadcast_in_dim_broadcast_in_dim_broadcast_in_dim.3), calls=%async_computation.3 | async-start | bytes 131072 | tf_op jit(solution)/shard_map/all_to_all | solution.py:48
  225.9 15.8 %all-to-all-start.1 = ((bf16[32,128,64]{1,2,0:T(8,128)(2,1)}), bf16[32,128,64]{1,2,0:T(8,128)(2,1)S(1)}, u32[]{:S(2)}, u32[]{:S(2)}) async-start(bf16[32,128,64]{1,2,0:T(8,128)(2,1)} %bitcast.17), calls=%async_computation.1 | async-start | bytes 1048576 | tf_op jit(solution)/shard_map/all_to_all | solution.py:122
Sparse Core Ops, SparseCore 0:
  10.8 93.1 all-gather.3
  161.5 94.6 all-gather.7
  258.3 73.9 all-gather.5
